TPU v7x, 32 devices: a whole 2x2x4 slice. The times are simulated.
32 devices in a mesh: facet: 8 (over z, x), col: 4 (over y, core).
Axes of the slice: x: 2, y: 2, z: 4, core: 2. Of those that a mesh axis runs over, the one named last changes fastest.
Arguments:
- strips: bfloat16 [32768, 512], P('facet', 'col'), may hold values from -6 to 6
- offsets: int32 [4, 8], P('col'), may hold values from 0 to 4095
- vis_subgrid: int32 [16384], P(('facet', 'col')), may hold values from 0 to 31, as said below
- vis_uv: int32 [16384], P(('facet', 'col')), may hold values from 0 to 262143
- observed: float32 [16384], P(('facet', 'col')), may hold values from -6 to 6
- weights: float32 [16384], P(('facet', 'col')), may hold values from 0.25 to 1
Outputs:
- facet_residual: float32 [32768, 512], P('facet', 'col')
Inputs may be any that keep to these rules, and one draw needn't show every extreme that they name: `vis_subgrid`: within each device's aligned block of 512 visibilities no subgrid is named more than 32 times, and one subgrid, the same for all blocks, is named exactly 32 times in every block.
All inputs are finite; a program needn't handle non-finite values.
Results may differ from a plain program's by a relative error of at most 0.01.
Values may be sent and summed in bfloat16 or wider, within the bound.
A program may use at most 128 MiB of HBM per device.

v0:
```python
import functools
import math

import jax
import jax.numpy as jnp
import numpy as np
from jax import lax
from jax.experimental import pallas as pl
from jax.experimental.pallas import tpu as pltpu
from jax.sharding import PartitionSpec as P

SG = 512
LANES = 128
VALS = 8


def cas_tables(rows_total, width):
    phase = np.arange(width)[:, None] * np.arange(rows_total)[None, :] % rows_total
    angle = 2.0 * np.pi * phase / rows_total
    taper = (0.6 - 0.4 * np.cos(2.0 * np.pi * np.arange(rows_total) / rows_total)) / math.sqrt(
        rows_total
    )
    cas = (np.cos(angle) + np.sin(angle)).astype(np.float32)
    dif = (np.cos(angle) - np.sin(angle)).astype(np.float32)
    return cas, dif, taper.astype(np.float32)[None, :]


def grid_tables(quarter, width, sub_size):
    phase = np.arange(sub_size)[:, None] * np.arange(sub_size)[None, :] % sub_size
    angle = 2.0 * np.pi * phase / sub_size
    cas = ((np.cos(angle) + np.sin(angle)) / math.sqrt(sub_size)).astype(jnp.bfloat16)
    start = np.arange(quarter) * sub_size // quarter
    target = (start[:, None] + np.arange(width)[None, :]).reshape(-1) % sub_size
    return cas, cas[target]


def sin_cos(turn):
    quad = jnp.floor(4.0 * turn + 0.5)
    x = (turn - 0.25 * quad) * (2.0 * math.pi)
    y = x * x
    s = x * (1.0 + y * (-1.0 / 6 + y * (1.0 / 120 + y * (-1.0 / 5040 + y * (1.0 / 362880)))))
    c = 1.0 + y * (-0.5 + y * (1.0 / 24 + y * (-1.0 / 720 + y * (1.0 / 40320))))
    one, two, three = quad == 1.0, quad == 2.0, quad == 3.0
    sine = jnp.where(one, c, jnp.where(two, -s, jnp.where(three, -c, s)))
    cosine = jnp.where(one, -s, jnp.where(two, -c, jnp.where(three, s, c)))
    return sine, cosine


def kernel(
    n, ncol, cap,
    strips, offs, vsub, vuv, obs, wts, cas, dif, taper, ctab, cplace,
    out,
    atab, cos_rows, sin_rows, vsend, vrecv, csend, crecv, rsend, rrecv,
    vis, hot_u, hot_v, hot_w, grid_s, grid_f, ret_t,
    vs_sem, vr_sem, cs_sem, cr_sem, rs_sem, rr_sem,
):
    rows_total, width = strips.shape
    devices = n * ncol
    quarter = n // 4
    nvis = vsub.shape[1]
    group = LANES // cap
    groups = devices // group
    me = lax.axis_index("facet")
    my_col = lax.axis_index("col")
    flat = me * ncol + my_col
    f32, bf16 = jnp.float32, jnp.bfloat16

    barrier = pltpu.get_barrier_semaphore()

    def greet(d, carry):
        t = lax.rem(flat + d, devices)
        pl.semaphore_signal(
            barrier, inc=1, device_id={"facet": t // ncol, "col": lax.rem(t, ncol)},
            device_id_type=pl.DeviceIdType.MESH,
        )
        return carry

    lax.fori_loop(1, devices, greet, 0)

    sub = vsub[...]
    hits = lax.broadcasted_iota(jnp.int32, (devices, nvis), 0) == sub
    hits_f = jnp.where(hits, 1.0, 0.0).astype(f32)
    before = (
        lax.broadcasted_iota(jnp.int32, (nvis, nvis), 0)
        < lax.broadcasted_iota(jnp.int32, (nvis, nvis), 1)
    )
    before = jnp.where(before, 1.0, 0.0).astype(bf16)
    counts = jnp.dot(hits_f.astype(bf16), before, preferred_element_type=f32)
    rank = jnp.sum(counts * hits_f, axis=0, keepdims=True)
    lane = rank + (lax.rem(flat, group) * cap).astype(f32)
    slots = lax.broadcasted_iota(jnp.int32, (LANES, nvis), 0).astype(f32) == lane
    slots = jnp.where(slots, 1.0, 0.0).astype(f32)
    uv = vuv[...]
    pu = (uv // SG).astype(f32)
    pv = (uv % SG).astype(f32)
    vals = jnp.concatenate(
        [pu, pv, obs[...], wts[...], jnp.zeros((VALS - 4, nvis), f32)], axis=0
    )
    left = hits_f[:, None, :] * vals[None, :, :]
    packed = lax.dot_general(
        left.reshape(devices * VALS, nvis), slots, (((1,), (1,)), ((), ())),
        precision=lax.Precision.HIGHEST, preferred_element_type=f32,
    )
    vsend[...] = packed.reshape(devices, VALS, LANES)
    vrecv[flat] = vsend[flat]

    row = lax.broadcasted_iota(jnp.int32, (n, rows_total), 1)
    turn = ((offs[...] * row) % rows_total).astype(f32) * (1.0 / rows_total)
    sine, cosine = sin_cos(turn)
    cos_rows[...] = (cosine * taper[...]).reshape(n, 1, rows_total)
    sin_rows[...] = (sine * taper[...]).reshape(n, 1, rows_total)

    pl.semaphore_wait(barrier, devices - 1)

    def vis_copy(to, source):
        return pltpu.make_async_remote_copy(
            src_ref=vsend.at[to], dst_ref=vrecv.at[source],
            send_sem=vs_sem.at[to], recv_sem=vr_sem.at[source],
            device_id={"facet": to // ncol, "col": lax.rem(to, ncol)},
            device_id_type=pl.DeviceIdType.MESH,
        )

    def block_copy(send, recv, s_sem, r_sem, to, source):
        return pltpu.make_async_remote_copy(
            src_ref=send.at[to], dst_ref=recv.at[source],
            send_sem=s_sem.at[to], recv_sem=r_sem.at[source],
            device_id={"facet": to}, device_id_type=pl.DeviceIdType.MESH,
        )

    def send_vis(d, carry):
        vis_copy(lax.rem(flat + d, devices), flat).start()
        return carry

    lax.fori_loop(1, devices, send_vis, 0)

    chunk = min(512, rows_total)

    def one_owner(i, carry):
        o = lax.rem(me + 1 + i, n)
        at = pl.ds(pl.multiple_of(o * width, width), width)
        acc = jnp.zeros((width, strips.shape[1]), f32)
        for c in range(rows_total // chunk):
            cols = pl.ds(c * chunk, chunk)
            mixed = cos_rows[o, :, cols] * cas[:, cols] + sin_rows[o, :, cols] * dif[:, cols]
            mixed = mixed.astype(bf16)
            atab[at, cols] = mixed
            acc = acc + jnp.dot(mixed, strips[cols, :], preferred_element_type=f32)
        csend[o] = acc.astype(bf16)

        @pl.when(i < n - 1)
        def _():
            block_copy(csend, crecv, cs_sem, cr_sem, o, me).start()

        return carry

    lax.fori_loop(0, n, one_owner, 0)
    crecv[me] = csend[me]

    def wait_vis(d, carry):
        vis_copy(flat, lax.rem(flat + d, devices)).wait_recv()
        return carry

    lax.fori_loop(1, devices, wait_vis, 0)
    for g in range(groups):
        vis[:, g * LANES:(g + 1) * LANES] = jnp.sum(vrecv[g * group:(g + 1) * group], axis=0)
    total = groups * LANES
    step = min(256, total)
    pixel = lax.broadcasted_iota(jnp.int32, (SG, step), 0).astype(f32)
    for v in range(total // step):
        span = slice(v * step, (v + 1) * step)
        hot_u[:, span] = jnp.where(pixel == vis[0:1, span], 1.0, 0.0).astype(bf16)
        hot_v[:, span] = jnp.where(pixel == vis[1:2, span], 1.0, 0.0).astype(bf16)

    def wait_block(send, recv, s_sem, r_sem):
        def body(d, carry):
            block_copy(send, recv, s_sem, r_sem, me, lax.rem(me + n - d, n)).wait_recv()
            return carry

        lax.fori_loop(1, n, body, 0)

    wait_block(csend, crecv, cs_sem, cr_sem)
    for f in range(n):
        q, b = f // 4, f % 4
        grid_s[b * width:(b + 1) * width, q * width:(q + 1) * width] = crecv[f]
    half = jnp.dot(ctab[...], grid_s[...], preferred_element_type=f32).astype(bf16)
    grid_f[...] = jnp.dot(half, cplace[...], preferred_element_type=f32).astype(bf16)

    def residual(v, carry):
        span = pl.ds(pl.multiple_of(v * step, step), step)
        rows = jnp.dot(grid_f[...], hot_v[:, span], preferred_element_type=f32)
        predicted = jnp.sum(rows * hot_u[:, span].astype(f32), axis=0, keepdims=True)
        weighted = vis[3:4, span] * (vis[2:3, span] - predicted)
        hot_w[:, span] = (hot_v[:, span].astype(f32) * weighted).astype(bf16)
        return carry

    lax.fori_loop(0, total // step, residual, 0)
    weight_t = lax.dot_general(
        hot_w[...], hot_u[...], (((1,), (1,)), ((), ())), preferred_element_type=f32
    ).astype(bf16)
    grid_g = jnp.dot(weight_t, ctab[...], preferred_element_type=f32).astype(bf16)
    for q in range(quarter):
        part = jnp.dot(
            cplace[q * width:(q + 1) * width, :], grid_g, preferred_element_type=f32
        )
        part = (part * math.sqrt(SG)).astype(bf16)
        for b in range(4):
            f = q * 4 + b
            rsend[f] = part[:, b * width:(b + 1) * width]

            @pl.when(me != f)
            def _():
                block_copy(rsend, rrecv, rs_sem, rr_sem, f, me).start()

    rrecv[me] = rsend[me]
    wait_block(rsend, rrecv, rs_sem, rr_sem)
    for f in range(n):
        ret_t[:, f * width:(f + 1) * width] = rrecv[f]

    def finish(c, carry):
        span = pl.ds(pl.multiple_of(c * chunk, chunk), chunk)
        part = jnp.dot(ret_t[...], atab[:, span], preferred_element_type=f32)
        out[span, :] = part.T
        return carry

    lax.fori_loop(0, rows_total // chunk, finish, 0)

    def sent_vis(d, carry):
        vis_copy(lax.rem(flat + d, devices), flat).wait_send()
        return carry

    lax.fori_loop(1, devices, sent_vis, 0)

    def sent_blocks(d, carry):
        to = lax.rem(me + d, n)
        block_copy(csend, crecv, cs_sem, cr_sem, to, me).wait_send()
        block_copy(rsend, rrecv, rs_sem, rr_sem, to, me).wait_send()
        return carry

    lax.fori_loop(1, n, sent_blocks, 0)


def solution(mesh):
    n, ncol = mesh.shape["facet"], mesh.shape["col"]
    devices = n * ncol

    def per_device(strips, offsets, vis_subgrid, vis_uv, observed, weights):
        rows_total, width = strips.shape
        nvis = vis_subgrid.shape[0]
        cap = 2 * nvis // devices
        quarter = n // 4
        total = devices * cap
        cas, dif, taper = cas_tables(rows_total, width)
        ctab, cplace = grid_tables(quarter, width, SG)
        f32, bf16 = jnp.float32, jnp.bfloat16
        return pl.pallas_call(
            functools.partial(kernel, n, ncol, cap),
            out_shape=jax.ShapeDtypeStruct((rows_total, width), f32),
            in_specs=[pl.BlockSpec(memory_space=pltpu.VMEM)] * 11,
            out_specs=pl.BlockSpec(memory_space=pltpu.VMEM),
            scratch_shapes=[
                pltpu.VMEM((n * width, rows_total), bf16),
                pltpu.VMEM((n, 1, rows_total), f32),
                pltpu.VMEM((n, 1, rows_total), f32),
                pltpu.VMEM((devices, VALS, LANES), f32),
                pltpu.VMEM((devices, VALS, LANES), f32),
                pltpu.VMEM((n, width, width), bf16),
                pltpu.VMEM((n, width, width), bf16),
                pltpu.VMEM((n, width, width), bf16),
                pltpu.VMEM((n, width, width), bf16),
                pltpu.VMEM((VALS, total), f32),
                pltpu.VMEM((SG, total), bf16),
                pltpu.VMEM((SG, total), bf16),
                pltpu.VMEM((SG, total), bf16),
                pltpu.VMEM((SG, quarter * width), bf16),
                pltpu.VMEM((SG, SG), bf16),
                pltpu.VMEM((width, n * width), bf16),
                pltpu.SemaphoreType.DMA((devices,)),
                pltpu.SemaphoreType.DMA((devices,)),
                pltpu.SemaphoreType.DMA((n,)),
                pltpu.SemaphoreType.DMA((n,)),
                pltpu.SemaphoreType.DMA((n,)),
                pltpu.SemaphoreType.DMA((n,)),
            ],
            compiler_params=pltpu.CompilerParams(
                collective_id=0, has_side_effects=True, vmem_limit_bytes=58 * 1024 * 1024
            ),
        )(
            strips, offsets.reshape(n, 1), vis_subgrid.reshape(1, nvis),
            vis_uv.reshape(1, nvis), observed.reshape(1, nvis), weights.reshape(1, nvis),
            jnp.asarray(cas), jnp.asarray(dif), jnp.asarray(taper),
            jnp.asarray(ctab), jnp.asarray(cplace),
        )

    in_specs = (
        P("facet", "col"),
        P("col", None),
        P(("facet", "col")),
        P(("facet", "col")),
        P(("facet", "col")),
        P(("facet", "col")),
    )
    return jax.shard_map(
        per_device, mesh=mesh, in_specs=in_specs, out_specs=P("facet", "col"), check_vma=False
    )
```

profile of v0, /device:TPU:0, one launch (start us, length us, event | category | flops | bytes accessed | tf_op | source)
XLA Modules:
  0.0 39.0 jit_solution(14660923462889436924)
XLA Ops:
  0.0 1.3 %copy.12.offs = s32[8,1]{1,0:T(8,128)} copy(s32[8,1]{0,1:T(1,128)} %bitcast.9) | data formatting | bytes 64 | tf_op jit(solution)/shard_map/reshape | solution.py:288
  1.3 34.6 %shard_map.109 = f32[4096,128]{1,0:T(8,128)} custom-call(bf16[4096,128]{1,0:T(8,128)(2,1)} %strips.1, s32[8,1]{1,0:T(8,128)} %copy.12.offs, s32[1,512]{1,0:T(1,128)} %bitcast.5, s32[1,512]{1,0:T(1,128)} %bitcast.6, f32[1,512]{1,0:T(1,128)} %bitcast.7, f32[1,512]{1,0:T(1,128)} %bitcast.8, f32[128,4096]{1,0:T(8,128)} %constant.10.clone.cas, ...), custom_call_target="tpu_custom_call" | custom-call | tf_op jit(solution)/shard_map/pallas_call | solution.py:255
  36.0 3.0 %copy.14 = f32[4096,128]{1,0:T(8,128)} copy(f32[4096,128]{1,0:T(8,128)} %shard_map.109) | data formatting | bytes 4194304
where the time goes:
time: 39.2 us; the launch traced here: 39 us
  Pallas kernels  34.6 us (88%)
  local copies, waits for them, and re-layouts  4.37 us (11%)
    pallas_call x1, Pallas kernels, per_device(): pl.pallas_call(functools.partial(kernel, n, ncol, cap), out_shape=jax.Sha...  34.6 us
    unnamed x1, local copies, waits for them, and re-layouts  3.05 us
    reshape x1, local copies, waits for them, and re-layouts, per_device(): offsets.reshape(n, 1)  1.32 us

commit v1 on v0

--- a/solution.py
+++ b/solution.py
@@ -49,10 +49,10 @@
 def kernel(
     n, ncol, cap,
     strips, offs, vsub, vuv, obs, wts, cas, dif, taper, ctab, cplace,
-    out,
+    a_out, ret_t,
     atab, cos_rows, sin_rows, vsend, vrecv, csend, crecv, rsend, rrecv,
-    vis, hot_u, hot_v, hot_w, grid_s, grid_f, ret_t,
-    vs_sem, vr_sem, cs_sem, cr_sem, rs_sem, rr_sem,
+    vis, hot_u, hot_v, hot_w, grid_s, grid_f,
+    vs_sem, vr_sem, cs_sem, cr_sem, rs_sem, rr_sem, a_sem,
 ):
     rows_total, width = strips.shape
     devices = n * ncol
@@ -105,7 +105,11 @@
     vrecv[flat] = vsend[flat]
 
     row = lax.broadcasted_iota(jnp.int32, (n, rows_total), 1)
-    turn = ((offs[...] * row) % rows_total).astype(f32) * (1.0 / rows_total)
+    same = (
+        lax.broadcasted_iota(jnp.int32, (n, n), 0) == lax.broadcasted_iota(jnp.int32, (n, n), 1)
+    )
+    shift = jnp.sum(jnp.where(same, offs[...], 0).astype(f32), axis=1, keepdims=True)
+    turn = ((shift.astype(jnp.int32) * row) % rows_total).astype(f32) * (1.0 / rows_total)
     sine, cosine = sin_cos(turn)
     cos_rows[...] = (cosine * taper[...]).reshape(n, 1, rows_total)
     sin_rows[...] = (sine * taper[...]).reshape(n, 1, rows_total)
@@ -135,17 +139,28 @@
 
     chunk = min(512, rows_total)
 
+    def table_copy(i):
+        o = lax.rem(me + 1 + i, n)
+        at = pl.ds(pl.multiple_of(o * width, width), width)
+        return pltpu.make_async_copy(atab.at[lax.rem(i, 2)], a_out.at[at], a_sem.at[o])
+
     def one_owner(i, carry):
         o = lax.rem(me + 1 + i, n)
-        at = pl.ds(pl.multiple_of(o * width, width), width)
+        slot = lax.rem(i, 2)
+
+        @pl.when(i >= 2)
+        def _():
+            table_copy(i - 2).wait()
+
         acc = jnp.zeros((width, strips.shape[1]), f32)
         for c in range(rows_total // chunk):
             cols = pl.ds(c * chunk, chunk)
             mixed = cos_rows[o, :, cols] * cas[:, cols] + sin_rows[o, :, cols] * dif[:, cols]
             mixed = mixed.astype(bf16)
-            atab[at, cols] = mixed
+            atab[slot, :, cols] = mixed
             acc = acc + jnp.dot(mixed, strips[cols, :], preferred_element_type=f32)
         csend[o] = acc.astype(bf16)
+        table_copy(i).start()
 
         @pl.when(i < n - 1)
         def _():
@@ -216,13 +231,8 @@
     for f in range(n):
         ret_t[:, f * width:(f + 1) * width] = rrecv[f]
 
-    def finish(c, carry):
-        span = pl.ds(pl.multiple_of(c * chunk, chunk), chunk)
-        part = jnp.dot(ret_t[...], atab[:, span], preferred_element_type=f32)
-        out[span, :] = part.T
-        return carry
-
-    lax.fori_loop(0, rows_total // chunk, finish, 0)
+    table_copy(n - 2).wait()
+    table_copy(n - 1).wait()
 
     def sent_vis(d, carry):
         vis_copy(lax.rem(flat + d, devices), flat).wait_send()
@@ -237,6 +247,10 @@
         return carry
 
     lax.fori_loop(1, n, sent_blocks, 0)
+
+
+def finish(ret_t, atab, out):
+    out[...] = jnp.dot(ret_t[...], atab[...], preferred_element_type=jnp.float32).T
 
 
 def solution(mesh):
@@ -252,13 +266,18 @@
         cas, dif, taper = cas_tables(rows_total, width)
         ctab, cplace = grid_tables(quarter, width, SG)
         f32, bf16 = jnp.float32, jnp.bfloat16
-        return pl.pallas_call(
+        tables, returned = pl.pallas_call(
             functools.partial(kernel, n, ncol, cap),
-            out_shape=jax.ShapeDtypeStruct((rows_total, width), f32),
+            out_shape=(
+                jax.ShapeDtypeStruct((n * width, rows_total), bf16),
+                jax.ShapeDtypeStruct((width, n * width), bf16),
+            ),
             in_specs=[pl.BlockSpec(memory_space=pltpu.VMEM)] * 11,
-            out_specs=pl.BlockSpec(memory_space=pltpu.VMEM),
+            out_specs=(
+                pl.BlockSpec(memory_space=pl.ANY), pl.BlockSpec(memory_space=pltpu.VMEM)
+            ),
             scratch_shapes=[
-                pltpu.VMEM((n * width, rows_total), bf16),
+                pltpu.VMEM((2, width, rows_total), bf16),
                 pltpu.VMEM((n, 1, rows_total), f32),
                 pltpu.VMEM((n, 1, rows_total), f32),
                 pltpu.VMEM((devices, VALS, LANES), f32),
@@ -273,23 +292,35 @@
                 pltpu.VMEM((SG, total), bf16),
                 pltpu.VMEM((SG, quarter * width), bf16),
                 pltpu.VMEM((SG, SG), bf16),
-                pltpu.VMEM((width, n * width), bf16),
                 pltpu.SemaphoreType.DMA((devices,)),
                 pltpu.SemaphoreType.DMA((devices,)),
                 pltpu.SemaphoreType.DMA((n,)),
                 pltpu.SemaphoreType.DMA((n,)),
                 pltpu.SemaphoreType.DMA((n,)),
                 pltpu.SemaphoreType.DMA((n,)),
+                pltpu.SemaphoreType.DMA((n,)),
             ],
             compiler_params=pltpu.CompilerParams(
-                collective_id=0, has_side_effects=True, vmem_limit_bytes=58 * 1024 * 1024
+                collective_id=0, has_side_effects=True, vmem_limit_bytes=36 * 1024 * 1024
             ),
         )(
-            strips, offsets.reshape(n, 1), vis_subgrid.reshape(1, nvis),
+            strips, offsets, vis_subgrid.reshape(1, nvis),
             vis_uv.reshape(1, nvis), observed.reshape(1, nvis), weights.reshape(1, nvis),
             jnp.asarray(cas), jnp.asarray(dif), jnp.asarray(taper),
             jnp.asarray(ctab), jnp.asarray(cplace),
         )
+        chunk = min(512, rows_total)
+        return pl.pallas_call(
+            finish,
+            out_shape=jax.ShapeDtypeStruct((rows_total, width), f32),
+            grid=(rows_total // chunk,),
+            in_specs=[
+                pl.BlockSpec((width, n * width), lambda i: (0, 0)),
+                pl.BlockSpec((n * width, chunk), lambda i: (0, i)),
+            ],
+            out_specs=pl.BlockSpec((chunk, width), lambda i: (i, 0)),
+            compiler_params=pltpu.CompilerParams(vmem_limit_bytes=20 * 1024 * 1024),
+        )(returned, tables)
 
     in_specs = (
         P("facet", "col"),

time: 39.2 us -> 43.6 us (1.11)
  local copies, waits for them, and re-layouts: 4.37 us -> 10.5 us
  Pallas kernels: 34.6 us -> 32.6 us
    unnamed x1 -> x22, local copies, waits for them, and re-layouts: 3.05 us -> 10.5 us
    pallas_call x1 -> x2, Pallas kernels: 34.6 us -> 32.6 us  [the longest x1 27.2 us: per_device(): pl.pallas_call(functools.partial(kernel, n, ncol, cap), out_shape=(jax.Sh...]
    reshape x1 -> x0, local copies, waits for them, and re-layouts: 1.32 us -> none  [per_device(): offsets.reshape(n, 1)]
where the time goes in v1:
time: 43.6 us; the launch traced here: 43.1 us
  Pallas kernels  32.6 us (75%)
  local copies, waits for them, and re-layouts  10.5 us (24%)
    pallas_call x1, Pallas kernels, per_device(): pl.pallas_call(functools.partial(kernel, n, ncol, cap), out_shape=(jax.Sh...  27.2 us
    unnamed x22, local copies, waits for them, and re-layouts  10.5 us
    pallas_call x1, Pallas kernels, per_device(): pl.pallas_call(finish, out_shape=jax.ShapeDtypeStruct((rows_total, width)...  5.38 us

profile of v1, /device:TPU:0, one launch (start us, length us, event | category | flops | bytes accessed | tf_op | source)
XLA Modules:
  0.0 43.1 jit_solution(16318958789027047674)
XLA Ops:
  0.0 0.0 copy-start
  0.0 1.6 %copy-done = f32[128,4096]{1,0:T(8,128)S(1)} copy-done((f32[128,4096]{1,0:T(8,128)S(1)}, f32[128,4096]{1,0:T(8,128)}, u32[]{:S(2)}) %copy-start) | copy-done | bytes 2097176
  1.6 0.0 copy-start.1
  1.6 1.6 %copy-done.1 = f32[128,4096]{1,0:T(8,128)S(1)} copy-done((f32[128,4096]{1,0:T(8,128)S(1)}, f32[128,4096]{1,0:T(8,128)}, u32[]{:S(2)}) %copy-start.1) | copy-done | bytes 2097176
  3.2 0.0 copy-start.2
  3.2 1.2 %copy-done.2 = bf16[4096,128]{1,0:T(8,128)(2,1)S(1)} copy-done((bf16[4096,128]{1,0:T(8,128)(2,1)S(1)}, bf16[4096,128]{1,0:T(8,128)(2,1)}, u32[]{:S(2)}) %copy-start.2) | copy-done | bytes 1048600
  4.4 0.0 copy-start.3
  4.4 1.0 %copy-done.3 = bf16[512,512]{1,0:T(8,128)(2,1)S(1)} copy-done((bf16[512,512]{1,0:T(8,128)(2,1)S(1)}, bf16[512,512]{1,0:T(8,128)(2,1)}, u32[]{:S(2)}) %copy-start.3) | copy-done | bytes 524312
  5.5 0.0 copy-start.4
  5.5 0.9 %copy-done.4 = bf16[256,512]{1,0:T(8,128)(2,1)S(1)} copy-done((bf16[256,512]{1,0:T(8,128)(2,1)S(1)}, bf16[256,512]{1,0:T(8,128)(2,1)}, u32[]{:S(2)}) %copy-start.4) | copy-done | bytes 262168
  6.4 0.0 copy-start.5
  6.4 0.7 %copy-done.5 = f32[1,4096]{1,0:T(1,128)S(1)} copy-done((f32[1,4096]{1,0:T(1,128)S(1)}, f32[1,4096]{1,0:T(1,128)}, u32[]{:S(2)}) %copy-start.5) | copy-done | bytes 16408
  7.1 0.0 copy-start.6
  7.1 0.7 %copy-done.6 = s32[512]{0:T(512)S(1)} copy-done((s32[512]{0:T(512)S(1)}, s32[512]{0:T(512)}, u32[]{:S(2)}) %copy-start.6) | copy-done | bytes 2072
  7.8 0.0 copy-start.7
  7.8 0.7 %copy-done.7 = s32[512]{0:T(512)S(1)} copy-done((s32[512]{0:T(512)S(1)}, s32[512]{0:T(512)}, u32[]{:S(2)}) %copy-start.7) | copy-done | bytes 2072
  8.5 0.0 copy-start.8
  8.5 0.7 %copy-done.8 = f32[512]{0:T(512)S(1)} copy-done((f32[512]{0:T(512)S(1)}, f32[512]{0:T(512)}, u32[]{:S(2)}) %copy-start.8) | copy-done | bytes 2072
  9.2 0.0 copy-start.9
  9.2 0.7 %copy-done.9 = f32[512]{0:T(512)S(1)} copy-done((f32[512]{0:T(512)S(1)}, f32[512]{0:T(512)}, u32[]{:S(2)}) %copy-start.9) | copy-done | bytes 2072
  9.8 0.0 copy-start.10
  9.8 0.7 %copy-done.10 = s32[1,8]{1,0:T(1,128)S(1)} copy-done((s32[1,8]{1,0:T(1,128)S(1)}, s32[1,8]{1,0:T(1,128)}, u32[]{:S(2)}) %copy-start.10) | copy-done | bytes 56
  10.5 27.2 %shard_map.109 = (bf16[1024,4096]{1,0:T(8,128)(2,1)S(1)}, bf16[128,1024]{1,0:T(8,128)(2,1)S(1)}) custom-call(bf16[4096,128]{1,0:T(8,128)(2,1)S(1)} %copy-done.2, s32[1,8]{1,0:T(1,128)S(1)} %copy-done.10, s32[1,512]{1,0:T(1,128)S(1)} %bitcast.4, s32[1,512]{1,0:T(1,128)S(1)} %bitcast.5, f32[1,512]{1,0:T(1,128)S(1)} %bitcast.6, f32[1,512]{1,0:T(1,128)S(1)} %bitcast.7, ...), custom_call_target="tpu_custom_call" | custom-call | tf_op jit(solution)/shard_map/pallas_call | solution.py:269
  37.7 5.4 %shard_map.110 = f32[4096,128]{1,0:T(8,128)} custom-call(bf16[128,1024]{1,0:T(8,128)(2,1)S(1)} %get-tuple-element.7.ret_t, bf16[1024,4096]{1,0:T(8,128)(2,1)S(1)} %get-tuple-element.8.atab), custom_call_target="tpu_custom_call" | custom-call | tf_op jit(solution)/shard_map/pallas_call | solution.py:313
Async XLA Ops:
  0.0 1.6 %copy-start = (f32[128,4096]{1,0:T(8,128)S(1)}, f32[128,4096]{1,0:T(8,128)}, u32[]{:S(2)}) copy-start(f32[128,4096]{1,0:T(8,128)} %constant.11.clone.dif) | copy-start | bytes 6291460
  1.6 1.6 %copy-start.1 = (f32[128,4096]{1,0:T(8,128)S(1)}, f32[128,4096]{1,0:T(8,128)}, u32[]{:S(2)}) copy-start(f32[128,4096]{1,0:T(8,128)} %constant.10.clone.cas) | copy-start | bytes 6291460
  3.2 1.2 %copy-start.2 = (bf16[4096,128]{1,0:T(8,128)(2,1)S(1)}, bf16[4096,128]{1,0:T(8,128)(2,1)}, u32[]{:S(2)}) copy-start(bf16[4096,128]{1,0:T(8,128)(2,1)} %strips.1) | copy-start | bytes 3145732
  4.4 1.0 %copy-start.3 = (bf16[512,512]{1,0:T(8,128)(2,1)S(1)}, bf16[512,512]{1,0:T(8,128)(2,1)}, u32[]{:S(2)}) copy-start(bf16[512,512]{1,0:T(8,128)(2,1)} %constant.13.clone.ctab) | copy-start | bytes 1572868
  5.5 0.9 %copy-start.4 = (bf16[256,512]{1,0:T(8,128)(2,1)S(1)}, bf16[256,512]{1,0:T(8,128)(2,1)}, u32[]{:S(2)}) copy-start(bf16[256,512]{1,0:T(8,128)(2,1)} %constant.14.clone.cplace) | copy-start | bytes 786436
  6.4 0.7 %copy-start.5 = (f32[1,4096]{1,0:T(1,128)S(1)}, f32[1,4096]{1,0:T(1,128)}, u32[]{:S(2)}) copy-start(f32[1,4096]{1,0:T(1,128)} %constant.12.clone.taper) | copy-start | bytes 49156
  7.1 0.7 %copy-start.6 = (s32[512]{0:T(512)S(1)}, s32[512]{0:T(512)}, u32[]{:S(2)}) copy-start(s32[512]{0:T(512)} %param.13) | copy-start | bytes 6148
  7.8 0.7 %copy-start.7 = (s32[512]{0:T(512)S(1)}, s32[512]{0:T(512)}, u32[]{:S(2)}) copy-start(s32[512]{0:T(512)} %param.14) | copy-start | bytes 6148
  8.5 0.7 %copy-start.8 = (f32[512]{0:T(512)S(1)}, f32[512]{0:T(512)}, u32[]{:S(2)}) copy-start(f32[512]{0:T(512)} %param.15) | copy-start | bytes 6148
  9.2 0.7 %copy-start.9 = (f32[512]{0:T(512)S(1)}, f32[512]{0:T(512)}, u32[]{:S(2)}) copy-start(f32[512]{0:T(512)} %param.16) | copy-start | bytes 6148
  9.8 0.7 %copy-start.10 = (s32[1,8]{1,0:T(1,128)S(1)}, s32[1,8]{1,0:T(1,128)}, u32[]{:S(2)}) copy-start(s32[1,8]{1,0:T(1,128)} %offs.1) | copy-start | bytes 100

commit v2 on v1

--- a/solution.py
+++ b/solution.py
@@ -48,11 +48,13 @@
 
 def kernel(
     n, ncol, cap,
-    strips, offs, vsub, vuv, obs, wts, cas, dif, taper, ctab, cplace,
+    strips_in, offs_in, vsub_in, vuv_in, obs_in, wts_in, cas_in, dif_in, taper_in, ctab_in,
+    cplace_in,
     a_out, ret_t,
     atab, cos_rows, sin_rows, vsend, vrecv, csend, crecv, rsend, rrecv,
     vis, hot_u, hot_v, hot_w, grid_s, grid_f,
     vs_sem, vr_sem, cs_sem, cr_sem, rs_sem, rr_sem, a_sem,
+    strips, offs, vsub, vuv, obs, wts, cas, dif, taper, ctab, cplace, in_sem,
 ):
     rows_total, width = strips.shape
     devices = n * ncol
@@ -65,6 +67,17 @@
     flat = me * ncol + my_col
     f32, bf16 = jnp.float32, jnp.bfloat16
 
+    loads = [
+        pltpu.make_async_copy(source, held, in_sem.at[at])
+        for at, (source, held) in enumerate([
+            (vsub_in, vsub), (vuv_in, vuv), (obs_in, obs), (wts_in, wts), (offs_in, offs),
+            (taper_in, taper), (cas_in, cas), (dif_in, dif), (strips_in, strips),
+            (ctab_in, ctab), (cplace_in, cplace),
+        ])
+    ]
+    for load in loads:
+        load.start()
+
     barrier = pltpu.get_barrier_semaphore()
 
     def greet(d, carry):
@@ -77,6 +90,8 @@
 
     lax.fori_loop(1, devices, greet, 0)
 
+    for load in loads[:4]:
+        load.wait()
     sub = vsub[...]
     hits = lax.broadcasted_iota(jnp.int32, (devices, nvis), 0) == sub
     hits_f = jnp.where(hits, 1.0, 0.0).astype(f32)
@@ -104,6 +119,8 @@
     vsend[...] = packed.reshape(devices, VALS, LANES)
     vrecv[flat] = vsend[flat]
 
+    for load in loads[4:6]:
+        load.wait()
     row = lax.broadcasted_iota(jnp.int32, (n, rows_total), 1)
     same = (
         lax.broadcasted_iota(jnp.int32, (n, n), 0) == lax.broadcasted_iota(jnp.int32, (n, n), 1)
@@ -137,6 +154,8 @@
 
     lax.fori_loop(1, devices, send_vis, 0)
 
+    for load in loads[6:9]:
+        load.wait()
     chunk = min(512, rows_total)
 
     def table_copy(i):
@@ -193,6 +212,8 @@
 
         lax.fori_loop(1, n, body, 0)
 
+    for load in loads[9:]:
+        load.wait()
     wait_block(csend, crecv, cs_sem, cr_sem)
     for f in range(n):
         q, b = f // 4, f % 4
@@ -272,7 +293,7 @@
                 jax.ShapeDtypeStruct((n * width, rows_total), bf16),
                 jax.ShapeDtypeStruct((width, n * width), bf16),
             ),
-            in_specs=[pl.BlockSpec(memory_space=pltpu.VMEM)] * 11,
+            in_specs=[pl.BlockSpec(memory_space=pl.ANY)] * 11,
             out_specs=(
                 pl.BlockSpec(memory_space=pl.ANY), pl.BlockSpec(memory_space=pltpu.VMEM)
             ),
@@ -299,9 +320,21 @@
                 pltpu.SemaphoreType.DMA((n,)),
                 pltpu.SemaphoreType.DMA((n,)),
                 pltpu.SemaphoreType.DMA((n,)),
+                pltpu.VMEM((rows_total, width), bf16),
+                pltpu.VMEM((1, n), jnp.int32),
+                pltpu.VMEM((1, nvis), jnp.int32),
+                pltpu.VMEM((1, nvis), jnp.int32),
+                pltpu.VMEM((1, nvis), f32),
+                pltpu.VMEM((1, nvis), f32),
+                pltpu.VMEM((width, rows_total), f32),
+                pltpu.VMEM((width, rows_total), f32),
+                pltpu.VMEM((1, rows_total), f32),
+                pltpu.VMEM((SG, SG), bf16),
+                pltpu.VMEM((quarter * width, SG), bf16),
+                pltpu.SemaphoreType.DMA((11,)),
             ],
             compiler_params=pltpu.CompilerParams(
-                collective_id=0, has_side_effects=True, vmem_limit_bytes=36 * 1024 * 1024
+                collective_id=0, has_side_effects=True, vmem_limit_bytes=58 * 1024 * 1024
             ),
         )(
             strips, offsets, vis_subgrid.reshape(1, nvis),
@@ -309,7 +342,7 @@
             jnp.asarray(cas), jnp.asarray(dif), jnp.asarray(taper),
             jnp.asarray(ctab), jnp.asarray(cplace),
         )
-        chunk = min(512, rows_total)
+        chunk = min(1024, rows_total)
         return pl.pallas_call(
             finish,
             out_shape=jax.ShapeDtypeStruct((rows_total, width), f32),
@@ -319,7 +352,7 @@
                 pl.BlockSpec((n * width, chunk), lambda i: (0, i)),
             ],
             out_specs=pl.BlockSpec((chunk, width), lambda i: (i, 0)),
-            compiler_params=pltpu.CompilerParams(vmem_limit_bytes=20 * 1024 * 1024),
+            compiler_params=pltpu.CompilerParams(vmem_limit_bytes=58 * 1024 * 1024),
         )(returned, tables)
 
     in_specs = (

time: 43.6 us -> 34.8 us (0.80)
  local copies, waits for them, and re-layouts: 10.5 us -> 0 us
  Pallas kernels: 32.6 us -> 34.6 us
    unnamed x22 -> x0, local copies, waits for them, and re-layouts: 10.5 us -> none
    pallas_call x1, Pallas kernels: 27.2 us -> 28.4 us  [per_device(): pl.pallas_call(functools.partial(kernel, n, ncol, cap), out_shape=(jax.Sh...]
    pallas_call x1, Pallas kernels: 5.38 us -> 6.21 us  [per_device(): pl.pallas_call(finish, out_shape=jax.ShapeDtypeStruct((rows_total, width)...]
where the time goes in v2:
time: 34.8 us; the launch traced here: 34.6 us
  Pallas kernels  34.6 us (99%)
    pallas_call x1, Pallas kernels, per_device(): pl.pallas_call(functools.partial(kernel, n, ncol, cap), out_shape=(jax.Sh...  28.4 us
    pallas_call x1, Pallas kernels, per_device(): pl.pallas_call(finish, out_shape=jax.ShapeDtypeStruct((rows_total, width)...  6.21 us

profile of v2, /device:TPU:0, one launch (start us, length us, event | category | flops | bytes accessed | tf_op | source)
XLA Modules:
  0.0 34.6 jit_solution(2457047865633925494)
XLA Ops:
  0.0 28.4 %shard_map.109 = (bf16[1024,4096]{1,0:T(8,128)(2,1)}, bf16[128,1024]{1,0:T(8,128)(2,1)}) custom-call(bf16[4096,128]{1,0:T(8,128)(2,1)} %strips_in.1, s32[1,8]{1,0:T(1,128)} %offs_in.1, s32[1,512]{1,0:T(1,128)} %bitcast.4, s32[1,512]{1,0:T(1,128)} %bitcast.5, f32[1,512]{1,0:T(1,128)} %bitcast.6, f32[1,512]{1,0:T(1,128)} %bitcast.7, ...), custom_call_target="tpu_custom_call" | custom-call | tf_op jit(solution)/shard_map/pallas_call | solution.py:290
  28.4 6.2 %shard_map.110 = f32[4096,128]{1,0:T(8,128)} custom-call(bf16[128,1024]{1,0:T(8,128)(2,1)} %get-tuple-element.7.ret_t, bf16[1024,4096]{1,0:T(8,128)(2,1)} %get-tuple-element.8.atab), custom_call_target="tpu_custom_call" | custom-call | tf_op jit(solution)/shard_map/pallas_call | solution.py:346

commit v3 on v2

--- a/solution.py
+++ b/solution.py
@@ -342,7 +342,7 @@
             jnp.asarray(cas), jnp.asarray(dif), jnp.asarray(taper),
             jnp.asarray(ctab), jnp.asarray(cplace),
         )
-        chunk = min(1024, rows_total)
+        chunk = min(2048, rows_total)
         return pl.pallas_call(
             finish,
             out_shape=jax.ShapeDtypeStruct((rows_total, width), f32),

time: 34.8 us -> 33.9 us (0.974)
  Pallas kernels: 34.6 us -> 33.7 us
    pallas_call x1, Pallas kernels: 6.21 us -> 5.36 us  [per_device(): pl.pallas_call(finish, out_shape=jax.ShapeDtypeStruct((rows_total, width)...]
where the time goes in v3:
time: 33.9 us; the launch traced here: 33.7 us
  Pallas kernels  33.7 us (99%)
    pallas_call x1, Pallas kernels, per_device(): pl.pallas_call(functools.partial(kernel, n, ncol, cap), out_shape=(jax.Sh...  28.4 us
    pallas_call x1, Pallas kernels, per_device(): pl.pallas_call(finish, out_shape=jax.ShapeDtypeStruct((rows_total, width)...  5.36 us

profile of v3, /device:TPU:0, one launch (start us, length us, event | category | flops | bytes accessed | tf_op | source)
XLA Modules:
  0.0 33.7 jit_solution(7567345566701062139)
XLA Ops:
  0.0 28.4 %shard_map.109 = (bf16[1024,4096]{1,0:T(8,128)(2,1)}, bf16[128,1024]{1,0:T(8,128)(2,1)}) custom-call(bf16[4096,128]{1,0:T(8,128)(2,1)} %strips_in.1, s32[1,8]{1,0:T(1,128)} %offs_in.1, s32[1,512]{1,0:T(1,128)} %bitcast.4, s32[1,512]{1,0:T(1,128)} %bitcast.5, f32[1,512]{1,0:T(1,128)} %bitcast.6, f32[1,512]{1,0:T(1,128)} %bitcast.7, ...), custom_call_target="tpu_custom_call" | custom-call | tf_op jit(solution)/shard_map/pallas_call | solution.py:290
  28.4 5.4 %shard_map.110 = f32[4096,128]{1,0:T(8,128)} custom-call(bf16[128,1024]{1,0:T(8,128)(2,1)} %get-tuple-element.7.ret_t, bf16[1024,4096]{1,0:T(8,128)(2,1)} %get-tuple-element.8.atab), custom_call_target="tpu_custom_call" | custom-call | tf_op jit(solution)/shard_map/pallas_call | solution.py:346
